TPU v7x, 512 devices: a whole 4x8x8 slice. The times are simulated.
512 devices in a mesh: dp: 32 (over z, x_hi, core), tensor: 16 (over x_lo, y).
Axes of the slice: x: 4 (x_hi: 2, x_lo: 2; x = x_hi * 2 + x_lo), y: 8, z: 8, core: 2. Of those that a mesh axis runs over, the one named last changes fastest.
Arguments:
- gate_pre: bfloat16 [4096, 14336], P('dp', 'tensor'), may hold values from -6 to 6
- up_pre: bfloat16 [4096, 14336], P('dp', 'tensor'), may hold values from -6 to 6
- cotangent: bfloat16 [4096, 4096], P('dp', 'tensor'), may hold values from -6 to 6
- weight_tiles: bfloat16 [16, 96, 128, 128], P('tensor', 'dp'), may hold values from -0.109375 to 0.109375
- tile_slots: int32 [16, 96], P('tensor', 'dp'), may hold values from 0 to 223, as said below
- live_counts: int32 [16], P('tensor'), may hold values from 24 to 96, as said below
Outputs:
- projected: bfloat16 [4096, 4096], P('dp', 'tensor')
- gate_grad: bfloat16 [4096, 14336], P('dp', 'tensor')
- up_grad: bfloat16 [4096, 14336], P('dp', 'tensor')
- tile_grad: float32 [16, 96, 128, 128], P('tensor', 'dp')
Inputs may be any that keep to these rules, and one draw needn't show every extreme that they name: `tile_slots`: within one tensor shard all 96 entries are distinct. `live_counts`: some shard has all 96 slots live.
All inputs are finite; a program needn't handle non-finite values.
Results may differ from a plain program's by a relative error of at most 0.019.
Values may be sent and summed in bfloat16 or wider, within the bound.
A program may use at most 64 MiB of HBM per device.

v0:
```python
import jax
import jax.numpy as jnp
from jax import lax
from jax.sharding import PartitionSpec as P


def per_device(gate_pre, up_pre, cotangent, weight_tiles, tile_slots, live_counts):
    tok_rows = gate_pre.shape[0]
    hid_width = gate_pre.shape[1]
    tile_edge = weight_tiles.shape[2]
    hid_blocks = hid_width // tile_edge
    shards = lax.axis_size("tensor")
    local_blocks = cotangent.shape[1] // tile_edge
    model_blocks = local_blocks * shards
    token_scale = (tok_rows * lax.axis_size("dp")) ** (-0.5)
    group_size = 16
    gate_val = gate_pre.astype(jnp.float32)
    up_val = up_pre.astype(jnp.float32)
    gate_sig = jax.nn.sigmoid(gate_val)
    silu_val = gate_val * gate_sig
    hidden = (silu_val * up_val).astype(jnp.bfloat16)
    hidden_blocks = hidden.reshape(tok_rows, hid_blocks, tile_edge).transpose(1, 0, 2)
    fetched_tiles, fetched_slots = (
        lax.all_gather(weight_tiles, "dp", axis=1, tiled=True),
        lax.all_gather(tile_slots, "dp", axis=1, tiled=True),
    )
    all_tiles = fetched_tiles[0]
    all_slots = fetched_slots[0]
    capacity = all_tiles.shape[0]
    live_count = live_counts[0]
    groups = capacity // group_size

    def forward_group(group_index, totals):
        offset = group_index * group_size
        group_tiles = lax.dynamic_slice_in_dim(all_tiles, offset, group_size, 0)
        group_slots = lax.dynamic_slice_in_dim(all_slots, offset, group_size, 0)
        is_live = offset + jnp.arange(group_size, dtype=jnp.int32) < live_count
        hid_index = group_slots // model_blocks
        mod_index = group_slots % model_blocks
        picked = hidden_blocks[hid_index]
        product = jnp.einsum(
            "gtb,gbc->gtc", picked, group_tiles, preferred_element_type=jnp.float32
        )
        product = jnp.where(is_live[:, None, None], product, 0.0)
        return totals.at[mod_index].add(product)

    sums = lax.fori_loop(
        0, groups, forward_group, jnp.zeros((model_blocks, tok_rows, tile_edge), jnp.float32)
    )
    shared = sums.astype(jnp.bfloat16).reshape(1, model_blocks, tok_rows, tile_edge)
    received = lax.all_to_all(shared, "tensor", split_axis=1, concat_axis=0, tiled=True)
    column_total = jnp.sum(received.astype(jnp.float32), axis=0)
    projected = (
        column_total.transpose(1, 0, 2)
        .reshape(tok_rows, local_blocks * tile_edge)
        .astype(jnp.bfloat16)
    )
    cot_local = cotangent.reshape(tok_rows, local_blocks, tile_edge).transpose(1, 0, 2)
    all_cot = lax.all_gather(cot_local, "tensor", axis=0, tiled=True)
    part_tiles = lax.all_gather(weight_tiles, "dp", axis=1, tiled=True)[0]
    part_slots = lax.all_gather(tile_slots, "dp", axis=1, tiled=True)[0]
    hidden_grad = jnp.zeros((hid_blocks, tok_rows, tile_edge), jnp.float32)
    grad_buffer = jnp.zeros((capacity, tile_edge, tile_edge), jnp.float32)
    count_here = part_tiles.shape[0]
    is_live = jnp.arange(count_here, dtype=jnp.int32) < live_count
    hid_index = part_slots // model_blocks
    mod_index = part_slots % model_blocks
    picked = hidden_blocks[hid_index]
    cot_picked = all_cot[mod_index]
    back = jnp.einsum("gtc,gbc->gtb", cot_picked, part_tiles, preferred_element_type=jnp.float32)
    back = jnp.where(is_live[:, None, None], back, 0.0)
    hidden_grad = hidden_grad.at[hid_index].add(back)
    tile_terms = (
        jnp.einsum("gtb,gtc->gbc", picked, cot_picked, preferred_element_type=jnp.float32)
        * token_scale
    )
    tile_terms = jnp.where(is_live[:, None, None], tile_terms, 0.0)
    grad_buffer = lax.dynamic_update_slice_in_dim(grad_buffer, tile_terms, jnp.int32(0), 0)
    hidden_grad, grad_buffer = (hidden_grad, grad_buffer)
    tile_grad = lax.psum_scatter(
        grad_buffer.reshape(1, capacity, tile_edge, tile_edge).astype(jnp.bfloat16),
        "dp",
        scatter_dimension=1,
        tiled=True,
    ).astype(jnp.float32)
    flat_grad = hidden_grad.transpose(1, 0, 2).reshape(tok_rows, hid_width)
    gate_grad = (flat_grad * up_val * gate_sig * (1.0 + gate_val * (1.0 - gate_sig))).astype(
        jnp.bfloat16
    )
    up_grad = (flat_grad * silu_val).astype(jnp.bfloat16)
    return (projected, gate_grad, up_grad, tile_grad)


def solution(mesh):
    in_specs = (
        P("dp", "tensor"),
        P("dp", "tensor"),
        P("dp", "tensor"),
        P("tensor", "dp", None, None),
        P("tensor", "dp"),
        P("tensor"),
    )
    out_specs = (
        P("dp", "tensor"),
        P("dp", "tensor"),
        P("dp", "tensor"),
        P("tensor", "dp", None, None),
    )
    return jax.shard_map(
        per_device, mesh=mesh, in_specs=in_specs, out_specs=out_specs, check_vma=False
    )
```

profile of v0, /device:TPU:8, one launch (start us, length us, event | category | flops | bytes accessed | tf_op | source)
XLA Modules:
  0.0 349.0 jit_solution(15729898504732721188)
XLA Ops:
  7.2 0.9 copy.40
  8.2 0.7 copy.41
  9.0 0.7 all-gather.3.cloned.1.call-update
  10.4 1.1 copy.35
  11.5 1.8 copy.36
  13.3 1.3 dynamic-slice
  15.2 0.8 bitcast_dynamic-update-slice_fusion
  15.9 24.1 %all-reduce = s32[96]{0:T(128)S(1)} all-reduce(s32[96]{0:T(128)S(1)} %bitcast_dynamic-update-slice_fusion), channel_id=1, replica_groups=mesh['dp'=32,'tensor'=16] {'dp'}, use_global_device_ids=true, to_apply=%add | all-reduce | flops 96 | bytes 768 | tf_op jit(solution)/shard_map/squeeze | solution.py:28
  40.1 45.9 %all-gather.5.cloned.1.call-done = bf16[32,128,128]{2,1,0:T(8,128)(2,1)} async-done(((bf16[2,128,128]{2,1,0:T(8,128)(2,1)}), bf16[32,128,128]{2,1,0:T(8,128)(2,1)}) %all-gather.5.cloned.1.call-update) | async-done | bytes 1048592 | tf_op jit(solution)/shard_map/all_gather | solution.py:59
  86.0 2.4 gather_fusion.1
  88.4 89.2 %all-gather.3.cloned.1.call-done = bf16[1,96,128,128]{3,2,0,1:T(8,128)(2,1)} async-done(((bf16[1,3,128,128]{3,2,0,1:T(8,128)(2,1)}), bf16[1,96,128,128]{3,2,0,1:T(8,128)(2,1)}) %all-gather.3.cloned.1.call-update) | async-done | bytes 3145744 | tf_op jit(solution)/shard_map/all_gather | solution.py:24
  177.6 6.8 %broadcast_select_fusion = f32[96,128,128]{2,1,0:T(8,128)} fusion(pred[96]{0:T(512)(128)(4,1)S(1)} %iota_compare_fusion, bf16[96,128,128]{2,1,0:T(8,128)(2,1)S(1)} %gather_fusion.1, bf16[1,96,128,128]{3,2,0,1:T(8,128)(2,1)} %all-gather.3.cloned.1.call-done), kind=kOutput, calls=%fused_computation.19 | convolution fusion | flops 404226048 | bytes 12583008 | tf_op jit(solution)/shard_map/gtc,gbc->gtb/dot_general | solution.py:70
  184.5 12.9 %scatter_fusion.1 = f32[7,128,128]{2,1,0:T(8,128)S(1)} fusion(f32[7,128,128]{2,1,0:T(8,128)S(1)} %broadcast_in_dim.84, s32[96]{0:T(128)S(1)} %get-tuple-element.220, f32[96,128,128]{2,1,0:T(8,128)} %broadcast_select_fusion), kind=kCustom, calls=%fused_computation.4 | custom fusion | flops 1572864 | bytes 18874752 | tf_op jit(solution)/shard_map/scatter-add | solution.py:72
  198.1 2.7 gather_fusion.2
  200.8 5.5 %fusion.2 = bf16[1,96,128,128]{3,2,1,0:T(8,128)(2,1)} fusion(pred[96]{0:T(512)(128)(4,1)S(1)} %iota_compare_fusion, bf16[96,128,128]{1,2,0:T(8,128)(2,1)} %gather_fusion.2, bf16[96,128,128]{2,1,0:T(8,128)(2,1)} %copy-done), kind=kOutput, calls=%fused_computation.18 | convolution fusion | flops 407371776 | bytes 9437280 | tf_op jit(solution)/shard_map/gtb,gtc->gbc/dot_general | solution.py:74
  206.3 1.6 broadcast_in_dim.83
  207.9 37.1 %while.15 = (s32[]{:T(128)}, f32[32,128,128]{2,1,0:T(8,128)}, s32[96]{0:T(128)S(1)}, s32[]{:T(128)}, bf16[7,128,128]{2,1,0:T(8,128)(2,1)S(1)}, /*index=5*/bf16[9...) while((s32[]{:T(128)}, f32[32,128,128]{2,1,0:T(8,128)}, s32[96]{0:T(128)S(1)}, ...), condition=%wide.region_2.3_spmd, body=%wide.region_0.2_spmd.sunk | while | flops 67634632 | bytes 6296259 | solution.py:47
  208.0 0.6 gather_fusion
  208.7 0.7 add_compare_fusion.2
  209.3 1.3 convolution_select_fusion.2
  210.7 3.4 scatter_fusion
  214.2 0.6 gather_fusion
  214.8 0.7 add_compare_fusion.2
  215.5 1.3 convolution_select_fusion.2
  216.9 3.4 scatter_fusion
  220.4 0.6 gather_fusion
  221.0 0.7 add_compare_fusion.2
  221.7 1.4 convolution_select_fusion.2
  223.1 3.4 scatter_fusion
  227.3 0.7 add_compare_fusion.2
  227.9 1.3 convolution_select_fusion.2
  229.3 3.4 scatter_fusion
  232.8 0.6 gather_fusion
  233.4 0.7 add_compare_fusion.2
  234.1 1.3 convolution_select_fusion.2
  235.5 3.4 scatter_fusion
  238.9 0.6 gather_fusion
  239.6 0.7 add_compare_fusion.2
  240.2 1.4 convolution_select_fusion.2
  241.6 3.4 scatter_fusion
  245.0 2.8 convert_bitcast_fusion
  247.8 7.3 %all-to-all-start = ((bf16[1,32,128,128]{3,2,0,1:T(8,128)(2,1)}), bf16[1,32,128,128]{3,2,0,1:T(8,128)(2,1)S(1)}, u32[]{:S(2)}, u32[]{:S(2)}) async-start(bf16[1,32,128,128]{3,2,0,1:T(8,128)(2,1)} %convert_bitcast_fusion), calls=%async_computation | async-start | bytes 2097152 | tf_op jit(solution)/shard_map/all_to_all | solution.py:51
  255.0 0.8 copy.44
  255.9 0.8 copy.45
  256.7 25.1 %all-to-all-done = bf16[1,32,128,128]{3,2,0,1:T(8,128)(2,1)S(1)} async-done(((bf16[1,32,128,128]{3,2,0,1:T(8,128)(2,1)}), bf16[1,32,128,128]{3,2,0,1:T(8,128)(2,1)S(1)}, u32[]{:S(2)}, u32[]{:S(2)}) %all-to-all-start) | async-done | bytes 1048608 | tf_op jit(solution)/shard_map/all_to_all | solution.py:51
  282.0 0.7 copy.43
  282.8 58.1 %reduce-scatter.2.cloned.1.call-done = bf16[1,3,128,128]{3,2,1,0:T(8,128)(2,1)} async-done(((bf16[1,96,128,128]{3,2,1,0:T(8,128)(2,1)}), bf16[1,3,128,128]{3,2,1,0:T(8,128)(2,1)}) %reduce-scatter.2.cloned.1.call-update) | async-done | bytes 98320 | tf_op jit(solution)/shard_map/reduce_scatter | solution.py:80
  340.9 1.6 convert_element_type.58
  (39 shorter events, 2.4 us)
Async XLA Ops:
  7.2 78.8 %all-gather.5.cloned.1.call-start = ((), (), s32[]{:S(2)}) async-start(), calls=%async_computation.3 | async-start | bytes 1114112 | tf_op jit(solution)/shard_map/all_gather | solution.py:59
  8.9 168.7 %all-gather.3.cloned.1.call-start = ((), (), s32[]{:S(2)}) async-start(), calls=%async_computation.2 | async-start | bytes 3244032 | tf_op jit(solution)/shard_map/all_gather | solution.py:24
  9.7 331.2 %reduce-scatter.2.cloned.1.call-start = ((), (), s32[]{:S(2)}) async-start(), calls=%async_computation.4 | async-start | bytes 3244032 | tf_op jit(solution)/shard_map/reduce_scatter | solution.py:80
  88.4 89.2 %copy-start = (bf16[96,128,128]{2,1,0:T(8,128)(2,1)}, bf16[96,128,128]{2,1,0:T(8,128)(2,1)S(1)}, u32[]{:S(2)}) copy-start(bf16[96,128,128]{2,1,0:T(8,128)(2,1)S(1)} %gather_fusion.1) | copy-start | bytes 9437188
  184.5 13.1 %copy-start.1 = (bf16[128,896]{0,1:T(8,128)(2,1)S(1)}, bf16[128,896]{0,1:T(8,128)(2,1)}, u32[]{:S(2)}) copy-start(bf16[128,896]{0,1:T(8,128)(2,1)} %copy.36) | copy-start | bytes 688132
  247.8 34.0 %all-to-all-start = ((bf16[1,32,128,128]{3,2,0,1:T(8,128)(2,1)}), bf16[1,32,128,128]{3,2,0,1:T(8,128)(2,1)S(1)}, u32[]{:S(2)}, u32[]{:S(2)}) async-start(bf16[1,32,128,128]{3,2,0,1:T(8,128)(2,1)} %convert_bitcast_fusion), calls=%async_computation | async-start | bytes 2097152 | tf_op jit(solution)/shard_map/all_to_all | solution.py:51
Sparse Core Ops, SparseCore 0:
  10.7 75.2 all-gather.4
  89.4 88.2 all-gather.2
  206.4 134.4 reduce-scatter.1
where the time goes:
time: 350 us; the launch traced here: 349 us
  waiting for transfers between devices  219 us (63%)
  other arithmetic  42.6 us (12%)
  blocking collectives  24.1 us (7%)
  matrix products  20.4 us (6%)
  local copies, waits for them, and re-layouts  20.1 us (6%)
  between operations  15.2 us (4%)
  starting transfers between devices  7.4 us (2%)
    all_gather x1, waiting for transfers between devices, per_device(): lax.all_gather(weight_tiles, 'dp', axis=1, tiled=True)  89.2 us
    reduce_scatter x1, waiting for transfers between devices, per_device(): lax.psum_scatter(grad_buffer.reshape(1, capacity, tile_edge, tile_edge).a...  58.1 us
    all_gather x1, waiting for transfers between devices, per_device(): all_cot = lax.all_gather(cot_local, 'tensor', axis=0, tiled=True)  45.9 us
    all_to_all x1, waiting for transfers between devices, per_device(): lax.all_to_all(shared, 'tensor', split_axis=1, concat_axis=0, tiled=True)  25.1 us
    squeeze x1, blocking collectives, per_device(): all_slots = fetched_slots[0]  24.1 us
    scatter-add x6, other arithmetic, forward_group(): return totals.at[mod_index].add(product)  20.4 us
    scatter-add x1, other arithmetic, per_device(): hidden_grad = hidden_grad.at[hid_index].add(back)  12.9 us
    unnamed x13, local copies, waits for them, and re-layouts  8.27 us
  transfers between devices with their start and end apart: 4, of which 4 were waited for; matrix products, arithmetic and copies ran while one was open for 15% of the time, Pallas kernels for 0%

commit v1 on v0

--- a/solution.py
+++ b/solution.py
@@ -56,7 +56,9 @@
         .astype(jnp.bfloat16)
     )
     cot_local = cotangent.reshape(tok_rows, local_blocks, tile_edge).transpose(1, 0, 2)
-    all_cot = lax.all_gather(cot_local, "tensor", axis=0, tiled=True)
+    all_cot = jnp.concatenate(
+        lax.all_to_all(jnp.stack([cot_local] * lax.axis_size("tensor")), "tensor", 0, 0), axis=0
+    )
     part_tiles = lax.all_gather(weight_tiles, "dp", axis=1, tiled=True)[0]
     part_slots = lax.all_gather(tile_slots, "dp", axis=1, tiled=True)[0]
     hidden_grad = jnp.zeros((hid_blocks, tok_rows, tile_edge), jnp.float32)

time: 350 us -> 281 us (0.80)
  waiting for transfers between devices: 219 us -> 143 us
  starting transfers between devices: 7.4 us -> 16.6 us
    all_gather x1 -> x0, waiting for transfers between devices: 45.9 us -> none  [per_device(): all_cot = lax.all_gather(cot_local, 'tensor', axis=0, tiled=True)]
    all_gather x1, waiting for transfers between devices: 89.2 us -> 59.1 us  [per_device(): lax.all_gather(weight_tiles, 'dp', axis=1, tiled=True)]
    all_to_all x0 -> x1, starting transfers between devices: none -> 9.26 us  [per_device(): lax.all_to_all(jnp.stack([cot_local] * lax.axis_size('tensor')), 'tensor'...]
    unnamed x13 -> x14, local copies, waits for them, and re-layouts: 8.27 us -> 4.15 us
  transfers between devices with their start and end apart: 4 -> 4, of which waited for: 4 -> 3; matrix products, arithmetic and copies ran while one was open for 15% -> 18% of each run, Pallas kernels for 0% -> 0%
where the time goes in v1:
time: 281 us; the launch traced here: 280 us
  waiting for transfers between devices  143 us (51%)
  other arithmetic  42.7 us (15%)
  blocking collectives  23.1 us (8%)
  matrix products  21.4 us (8%)
  local copies, waits for them, and re-layouts  17.6 us (6%)
  starting transfers between devices  16.6 us (6%)
  between operations  15.5 us (6%)
    all_gather x1, waiting for transfers between devices, per_device(): lax.all_gather(weight_tiles, 'dp', axis=1, tiled=True)  59.1 us
    reduce_scatter x1, waiting for transfers between devices, per_device(): lax.psum_scatter(grad_buffer.reshape(1, capacity, tile_edge, tile_edge).a...  58.2 us
    all_to_all x1, waiting for transfers between devices, per_device(): lax.all_to_all(shared, 'tensor', split_axis=1, concat_axis=0, tiled=True)  25.1 us
    squeeze x1, blocking collectives, per_device(): all_slots = fetched_slots[0]  23.1 us
    scatter-add x6, other arithmetic, forward_group(): return totals.at[mod_index].add(product)  20.4 us
    scatter-add x1, other arithmetic, per_device(): hidden_grad = hidden_grad.at[hid_index].add(back)  12.9 us
    all_to_all x1, starting transfers between devices, per_device(): lax.all_to_all(jnp.stack([cot_local] * lax.axis_size('tensor')), 'tensor'...  9.26 us
    dot_general x6, matrix products, forward_group(): jnp.einsum('gtb,gbc->gtc', picked, group_tiles, preferred_element_type=jn...  8.08 us
  transfers between devices with their start and end apart: 4, of which 3 were waited for; matrix products, arithmetic and copies ran while one was open for 18% of the time, Pallas kernels for 0%

profile of v1, /device:TPU:8, one launch (start us, length us, event | category | flops | bytes accessed | tf_op | source)
XLA Modules:
  0.0 280.1 jit_solution(7043800576689017682)
XLA Ops:
  7.2 0.7 all-gather.2.cloned.1.call-update
  7.9 0.9 reshape.165
  8.8 1.2 stack.2
  10.0 9.3 %all-to-all-start.1 = ((bf16[16,2,128,128]{3,2,1,0:T(8,128)(2,1)}), bf16[16,2,128,128]{3,2,1,0:T(8,128)(2,1)S(1)}, u32[]{:S(2)}, u32[]{:S(2)}) async-start(bf16[16,2,128,128]{3,2,1,0:T(8,128)(2,1)} %stack.2), calls=%async_computation.1 | async-start | bytes 2097152 | tf_op jit(solution)/shard_map/all_to_all | solution.py:60
  20.4 1.3 dynamic-slice
  22.4 23.1 %all-reduce = s32[96]{0:T(128)S(1)} all-reduce(s32[96]{0:T(128)S(1)} %bitcast_dynamic-update-slice_fusion), channel_id=1, replica_groups=mesh['dp'=32,'tensor'=16] {'dp'}, use_global_device_ids=true, to_apply=%add | all-reduce | flops 96 | bytes 768 | tf_op jit(solution)/shard_map/squeeze | solution.py:28
  45.5 2.7 gather_fusion.1
  48.2 59.1 %all-gather.2.cloned.1.call-done = bf16[1,96,128,128]{3,2,0,1:T(8,128)(2,1)} async-done(((bf16[1,3,128,128]{3,2,0,1:T(8,128)(2,1)}), bf16[1,96,128,128]{3,2,0,1:T(8,128)(2,1)}) %all-gather.2.cloned.1.call-update) | async-done | bytes 3145744 | tf_op jit(solution)/shard_map/all_gather | solution.py:24
  107.4 7.8 %broadcast_select_fusion = f32[96,128,128]{2,1,0:T(8,128)} fusion(pred[96]{0:T(512)(128)(4,1)S(1)} %iota_compare_fusion, bf16[96,128,128]{2,1,0:T(8,128)(2,1)} %gather_fusion.1, bf16[1,96,128,128]{3,2,0,1:T(8,128)(2,1)} %all-gather.2.cloned.1.call-done), kind=kOutput, calls=%fused_computation.19 | convolution fusion | flops 404226048 | bytes 12583008 | tf_op jit(solution)/shard_map/gtc,gbc->gtb/dot_general | solution.py:72
  115.2 12.9 %scatter_fusion.1 = f32[7,128,128]{2,1,0:T(8,128)S(1)} fusion(f32[7,128,128]{2,1,0:T(8,128)S(1)} %broadcast_in_dim.84, s32[96]{0:T(128)S(1)} %get-tuple-element.210, f32[96,128,128]{2,1,0:T(8,128)} %broadcast_select_fusion), kind=kCustom, calls=%fused_computation.4 | custom fusion | flops 1572864 | bytes 18874752 | tf_op jit(solution)/shard_map/scatter-add | solution.py:74
  128.1 0.2 copy.34
  128.3 0.3 fusion.11
  128.8 2.7 gather_fusion.2
  131.5 5.5 %fusion.2 = bf16[1,96,128,128]{3,2,1,0:T(8,128)(2,1)} fusion(pred[96]{0:T(512)(128)(4,1)S(1)} %iota_compare_fusion, bf16[96,128,128]{1,2,0:T(8,128)(2,1)} %gather_fusion.2, bf16[96,128,128]{2,1,0:T(8,128)(2,1)} %gather_fusion.1), kind=kOutput, calls=%fused_computation.18 | convolution fusion | flops 407371776 | bytes 9437280 | tf_op jit(solution)/shard_map/gtb,gtc->gbc/dot_general | solution.py:76
  137.0 1.6 broadcast_in_dim.83
  138.6 37.1 %while.15 = (s32[]{:T(128)}, f32[32,128,128]{2,1,0:T(8,128)}, s32[96]{0:T(128)S(1)}, s32[]{:T(128)}, bf16[7,128,128]{2,1,0:T(8,128)(2,1)S(1)}, /*index=5*/bf16[9...) while((s32[]{:T(128)}, f32[32,128,128]{2,1,0:T(8,128)}, s32[96]{0:T(128)S(1)}, ...), condition=%wide.region_2.3_spmd, body=%wide.region_0.2_spmd.sunk | while | flops 67634632 | bytes 6296259 | solution.py:47
  138.7 0.6 gather_fusion
  139.3 0.7 add_compare_fusion.2
  140.0 1.3 convolution_select_fusion.2
  141.4 3.4 %scatter_fusion = f32[32,128,128]{2,1,0:T(8,128)} fusion(f32[32,128,128]{2,1,0:T(8,128)} %get-tuple-element.263, s32[16]{0:T(128)S(1)} %compare_select_fusion.14, f32[16,128,128]{2,1,0:T(8,128)S(1)} %convolution_select_fusion.2), kind=kCustom, calls=%fused_computation.3.clone.1 | custom fusion | flops 262144 | bytes 3145792 | tf_op jit(solution)/shard_map/while/body/eval_jaxpr/scatter-add | solution.py:45
  144.9 0.6 gather_fusion
  145.5 0.7 add_compare_fusion.2
  146.2 1.3 convolution_select_fusion.2
  147.5 3.4 %scatter_fusion = f32[32,128,128]{2,1,0:T(8,128)} fusion(f32[32,128,128]{2,1,0:T(8,128)} %get-tuple-element.263, s32[16]{0:T(128)S(1)} %compare_select_fusion.14, f32[16,128,128]{2,1,0:T(8,128)S(1)} %convolution_select_fusion.2), kind=kCustom, calls=%fused_computation.3.clone.1 | custom fusion | flops 262144 | bytes 3145792 | tf_op jit(solution)/shard_map/while/body/eval_jaxpr/scatter-add | solution.py:45
  151.1 0.6 gather_fusion
  151.7 0.7 add_compare_fusion.2
  152.4 1.4 convolution_select_fusion.2
  153.8 3.4 %scatter_fusion = f32[32,128,128]{2,1,0:T(8,128)} fusion(f32[32,128,128]{2,1,0:T(8,128)} %get-tuple-element.263, s32[16]{0:T(128)S(1)} %compare_select_fusion.14, f32[16,128,128]{2,1,0:T(8,128)S(1)} %convolution_select_fusion.2), kind=kCustom, calls=%fused_computation.3.clone.1 | custom fusion | flops 262144 | bytes 3145792 | tf_op jit(solution)/shard_map/while/body/eval_jaxpr/scatter-add | solution.py:45
  157.3 0.6 gather_fusion
  157.9 0.7 add_compare_fusion.2
  158.6 1.3 convolution_select_fusion.2
  160.0 3.4 %scatter_fusion = f32[32,128,128]{2,1,0:T(8,128)} fusion(f32[32,128,128]{2,1,0:T(8,128)} %get-tuple-element.263, s32[16]{0:T(128)S(1)} %compare_select_fusion.14, f32[16,128,128]{2,1,0:T(8,128)S(1)} %convolution_select_fusion.2), kind=kCustom, calls=%fused_computation.3.clone.1 | custom fusion | flops 262144 | bytes 3145792 | tf_op jit(solution)/shard_map/while/body/eval_jaxpr/scatter-add | solution.py:45
  163.5 0.6 gather_fusion
  164.1 0.7 add_compare_fusion.2
  164.8 1.3 convolution_select_fusion.2
  166.1 3.4 %scatter_fusion = f32[32,128,128]{2,1,0:T(8,128)} fusion(f32[32,128,128]{2,1,0:T(8,128)} %get-tuple-element.263, s32[16]{0:T(128)S(1)} %compare_select_fusion.14, f32[16,128,128]{2,1,0:T(8,128)S(1)} %convolution_select_fusion.2), kind=kCustom, calls=%fused_computation.3.clone.1 | custom fusion | flops 262144 | bytes 3145792 | tf_op jit(solution)/shard_map/while/body/eval_jaxpr/scatter-add | solution.py:45
  169.6 0.6 gather_fusion
  170.3 0.7 add_compare_fusion.2
  170.9 1.4 convolution_select_fusion.2
  172.3 3.4 %scatter_fusion = f32[32,128,128]{2,1,0:T(8,128)} fusion(f32[32,128,128]{2,1,0:T(8,128)} %get-tuple-element.263, s32[16]{0:T(128)S(1)} %compare_select_fusion.14, f32[16,128,128]{2,1,0:T(8,128)S(1)} %convolution_select_fusion.2), kind=kCustom, calls=%fused_computation.3.clone.1 | custom fusion | flops 262144 | bytes 3145792 | tf_op jit(solution)/shard_map/while/body/eval_jaxpr/scatter-add | solution.py:45
  175.7 2.8 convert_bitcast_fusion
  178.4 7.3 %all-to-all-start = ((bf16[1,32,128,128]{3,2,0,1:T(8,128)(2,1)}), bf16[1,32,128,128]{3,2,0,1:T(8,128)(2,1)S(1)}, u32[]{:S(2)}, u32[]{:S(2)}) async-start(bf16[1,32,128,128]{3,2,0,1:T(8,128)(2,1)} %convert_bitcast_fusion), calls=%async_computation | async-start | bytes 2097152 | tf_op jit(solution)/shard_map/all_to_all | solution.py:51
  185.7 0.8 copy.36
  186.5 0.8 copy.37
  187.4 25.1 %all-to-all-done = bf16[1,32,128,128]{3,2,0,1:T(8,128)(2,1)S(1)} async-done(((bf16[1,32,128,128]{3,2,0,1:T(8,128)(2,1)}), bf16[1,32,128,128]{3,2,0,1:T(8,128)(2,1)S(1)}, u32[]{:S(2)}, u32[]{:S(2)}) %all-to-all-start) | async-done | bytes 1048608 | tf_op jit(solution)/shard_map/all_to_all | solution.py:51
  212.7 0.7 copy.35
  213.5 58.2 %reduce-scatter.2.cloned.1.call-done = bf16[1,3,128,128]{3,2,1,0:T(8,128)(2,1)} async-done(((bf16[1,96,128,128]{3,2,1,0:T(8,128)(2,1)}), bf16[1,3,128,128]{3,2,1,0:T(8,128)(2,1)}) %reduce-scatter.2.cloned.1.call-update) | async-done | bytes 98320 | tf_op jit(solution)/shard_map/reduce_scatter | solution.py:82
  271.6 1.6 convert_element_type.58
  (41 shorter events, 1.7 us)
Async XLA Ops:
  7.2 12.8 %copy-start = (bf16[128,896]{1,0:T(8,128)(2,1)S(1)}, bf16[128,896]{1,0:T(8,128)(2,1)}, u32[]{:S(2)}) copy-start(bf16[128,896]{1,0:T(8,128)(2,1)} %param.8) | copy-start | bytes 688132
  7.2 13.0 %copy-start.1 = (bf16[128,896]{1,0:T(8,128)(2,1)S(1)}, bf16[128,896]{1,0:T(8,128)(2,1)}, u32[]{:S(2)}) copy-start(bf16[128,896]{1,0:T(8,128)(2,1)} %param.9) | copy-start | bytes 688132
  7.2 15.1 %copy-start.2 = (s32[1,3]{1,0:T(1,128)S(1)}, s32[1,3]{1,0:T(1,128)}, u32[]{:S(2)}) copy-start(s32[1,3]{1,0:T(1,128)} %param.12) | copy-start | bytes 40
  7.2 100.2 %all-gather.2.cloned.1.call-start = ((), (), s32[]{:S(2)}) async-start(), calls=%async_computation.3 | async-start | bytes 3244032 | tf_op jit(solution)/shard_map/all_gather | solution.py:24
  10.0 35.5 %all-to-all-start.1 = ((bf16[16,2,128,128]{3,2,1,0:T(8,128)(2,1)}), bf16[16,2,128,128]{3,2,1,0:T(8,128)(2,1)S(1)}, u32[]{:S(2)}, u32[]{:S(2)}) async-start(bf16[16,2,128,128]{3,2,1,0:T(8,128)(2,1)} %stack.2), calls=%async_computation.1 | async-start | bytes 2097152 | tf_op jit(solution)/shard_map/all_to_all | solution.py:60
  19.3 252.4 %reduce-scatter.2.cloned.1.call-start = ((), (), s32[]{:S(2)}) async-start(), calls=%async_computation.4 | async-start | bytes 3244032 | tf_op jit(solution)/shard_map/reduce_scatter | solution.py:82
  178.4 34.0 %all-to-all-start = ((bf16[1,32,128,128]{3,2,0,1:T(8,128)(2,1)}), bf16[1,32,128,128]{3,2,0,1:T(8,128)(2,1)S(1)}, u32[]{:S(2)}, u32[]{:S(2)}) async-start(bf16[1,32,128,128]{3,2,0,1:T(8,128)(2,1)} %convert_bitcast_fusion), calls=%async_computation | async-start | bytes 2097152 | tf_op jit(solution)/shard_map/all_to_all | solution.py:51
Sparse Core Ops, SparseCore 0:
  11.4 95.9 all-gather.1
  137.1 134.4 reduce-scatter.1
